TPU v7x, 512 devices: a whole 4x8x8 slice. The times are simulated.
512 devices in a mesh: dp: 32 (over y_hi, z, core), fsdp: 16 (over x, y_lo).
Axes of the slice: x: 4, y: 8 (y_hi: 2, y_lo: 4; y = y_hi * 4 + y_lo), z: 8, core: 2. Of those that a mesh axis runs over, the one named last changes fastest.
Arguments:
- inputs: bfloat16 [4096, 8192], P('fsdp', 'dp'), may hold values from -6 to 6
- cotangent: bfloat16 [4096, 14336], P('fsdp', 'dp'), may hold values from -6 to 6
- weight: bfloat16 [8192, 14336], P('dp', 'fsdp'), may hold values from -0.046875 to 0.046875
- projector: bfloat16 [8192, 512], P('dp'), may hold values from -0.25 to 0.25
- first_moment: float32 [512, 14336], P('dp', 'fsdp'), may hold values from -384 to 384
- second_moment: float32 [512, 14336], P('dp', 'fsdp'), may hold values from 327.68 to 13107.2
Outputs:
- input_grad: bfloat16 [4096, 8192], P('fsdp', 'dp')
- update: bfloat16 [8192, 14336], P('dp', 'fsdp')
All inputs are finite; a program needn't handle non-finite values.
Results may differ from a plain program's by a relative error of at most 0.0052.
Values may be sent and summed in bfloat16 or wider, within the bound.
A program may use at most 64 MiB of HBM per device.

v0:
```python
import jax
import jax.numpy as jnp
from jax import lax
from jax.sharding import PartitionSpec as P

decay_first = 0.9
decay_second = 0.999
bias_first = 0.9999734386
bias_second = 0.0952078528
epsilon_value = 1e-08


def contract_cols(left, right):
    return lax.dot_general(
        left, right, (((1,), (1,)), ((), ())), preferred_element_type=jnp.float32
    )


def contract_rows(left, right):
    return lax.dot_general(
        left, right, (((0,), (0,)), ((), ())), preferred_element_type=jnp.float32
    )


def body(inputs, cotangent, weight, projector, first_moment, second_moment):
    rank_share = first_moment.shape[0]
    partial_proj = jnp.dot(inputs, projector, preferred_element_type=jnp.float32)
    rank_offset = lax.axis_index("dp") * rank_share
    projected = lax.psum(partial_proj, "dp").astype(jnp.bfloat16)
    own_cols = lax.dynamic_slice_in_dim(projected, rank_offset, rank_share, 1)
    weight_full = lax.all_gather(weight, "fsdp", axis=1, tiled=True)
    portion = lax.all_gather(cotangent, "dp", axis=1, tiled=True)
    grad_in = contract_cols(portion, weight_full)
    grad_part = contract_rows(own_cols, portion)
    gradient = lax.psum_scatter(grad_part, "fsdp", scatter_dimension=1, tiled=True)
    moment_one = decay_first * first_moment + (1.0 - decay_first) * gradient
    moment_two = decay_second * second_moment + (1.0 - decay_second) * gradient * gradient
    direction = (
        moment_one / bias_first / (jnp.sqrt(moment_two / bias_second) + epsilon_value)
    ).astype(jnp.bfloat16)
    update = jnp.dot(
        projector,
        lax.all_gather(direction, "dp", axis=0, tiled=True),
        preferred_element_type=jnp.float32,
    )
    return (grad_in.astype(jnp.bfloat16), update.astype(jnp.bfloat16))


def solution(mesh):
    return jax.shard_map(
        body,
        mesh=mesh,
        in_specs=(
            P("fsdp", "dp"),
            P("fsdp", "dp"),
            P("dp", "fsdp"),
            P("dp", None),
            P("dp", "fsdp"),
            P("dp", "fsdp"),
        ),
        out_specs=(P("fsdp", "dp"), P("dp", "fsdp")),
        check_vma=False,
    )
```

profile of v0, /device:TPU:1, one launch (start us, length us, event | category | flops | bytes accessed | tf_op | source)
XLA Modules:
  0.0 464.3 jit_solution(16845197125807295108)
XLA Ops:
  7.2 0.0 copy-start
  7.2 0.0 all-gather.3.cloned.1.call-start
  7.2 0.7 all-gather.3.cloned.1.call-update
  7.9 0.0 all-gather.5.cloned.1.call-start
  8.0 0.7 all-gather.5.cloned.1.call-update
  8.7 0.0 reduce-scatter.2.cloned.1.call-start
  8.7 0.0 copy-done
  8.7 1.1 fusion.9
  9.9 187.7 %all-reduce.1 = bf16[256,512]{1,0:T(8,128)(2,1)S(1)} all-reduce(f32[256,512]{1,0:T(8,128)S(1)} %fusion.9), channel_id=1, replica_groups=mesh['dp'=32,'fsdp'=16] {'dp'}, use_global_device_ids=true, to_apply=%region_0.0 | all-reduce | flops 131072 | bytes 786432 | tf_op jit(solution)/shard_map/psum | solution.py:29
  197.5 0.0 all-gather.3.cloned.1.call-done
  197.6 6.2 %fusion.1 = f32[16,14336]{1,0:T(8,128)} fusion(bf16[256,14336]{0,1:T(8,128)(2,1)} %all-gather.3.cloned.1.call-done, bf16[256,512]{1,0:T(8,128)(2,1)S(1)} %all-reduce.1, s32[]{:T(128)S(6)} %select_n.3), kind=kOutput, calls=%fused_computation.5 | convolution fusion | flops 117440512 | bytes 8323076 | tf_op jit(solution)/shard_map/dot_general | solution.py:20
  203.7 0.0 reduce-scatter.2.cloned.1.call-update
  203.8 0.0 copy-start.1
  203.8 0.0 copy-start.2
  203.8 109.4 %all-gather.5.cloned.1.call-done = bf16[256,14336]{1,0:T(8,128)(2,1)} async-done(((bf16[256,896]{1,0:T(8,128)(2,1)}), bf16[256,14336]{1,0:T(8,128)(2,1)}) %all-gather.5.cloned.1.call-update) | async-done | bytes 7340048 | tf_op jit(solution)/shard_map/all_gather | solution.py:31
  313.2 7.9 %convolution_convert_fusion.1 = bf16[256,256]{1,0:T(8,128)(2,1)} fusion(bf16[256,14336]{0,1:T(8,128)(2,1)} %all-gather.3.cloned.1.call-done, bf16[256,14336]{1,0:T(8,128)(2,1)} %all-gather.5.cloned.1.call-done), kind=kOutput, calls=%fused_computation.2 | convolution fusion | flops 1879113728 | bytes 14811136 | tf_op jit(solution)/shard_map/dot_general | solution.py:14
  321.2 67.9 %reduce-scatter.2.cloned.1.call-done = f32[16,896]{1,0:T(8,128)} async-done(((f32[16,14336]{1,0:T(8,128)}), f32[16,896]{1,0:T(8,128)}) %reduce-scatter.2.cloned.1.call-update) | async-done | bytes 57360 | tf_op jit(solution)/shard_map/reduce_scatter | solution.py:35
  389.0 0.0 copy-done.1
  389.0 0.0 copy-done.2
  389.0 0.9 fusion.7
  389.9 66.4 %all_gather.11 = bf16[512,896]{1,0:T(8,128)(2,1)S(1)} all-gather(bf16[16,896]{1,0:T(8,128)(2,1)S(1)} %fusion.7), channel_id=1, replica_groups=mesh['dp'=32,'fsdp'=16] {'dp'}, dimensions={0}, use_global_device_ids=true | all-gather | bytes 946176 | tf_op jit(solution)/shard_map/all_gather | solution.py:43
  456.4 0.4 fusion
  456.8 1.0 copy.8
Async XLA Ops:
  7.2 1.6 copy-start
  7.2 190.4 %all-gather.3.cloned.1.call-start = ((), (), s32[]{:S(2)}) async-start(), calls=%async_computation.1 | async-start | bytes 7569408 | tf_op jit(solution)/shard_map/all_gather | solution.py:32
  7.9 305.3 %all-gather.5.cloned.1.call-start = ((), (), s32[]{:S(2)}) async-start(), calls=%async_computation.2 | async-start | bytes 7798784 | tf_op jit(solution)/shard_map/all_gather | solution.py:31
  8.7 380.4 %reduce-scatter.2.cloned.1.call-start = ((), (), s32[]{:S(2)}) async-start(), calls=%async_computation.3 | async-start | bytes 974848 | tf_op jit(solution)/shard_map/reduce_scatter | solution.py:35
  203.8 185.3 %copy-start.1 = (f32[16,896]{1,0:T(8,128)S(1)}, f32[16,896]{1,0:T(8,128)}, u32[]{:S(2)}) copy-start(f32[16,896]{1,0:T(8,128)} %param.11) | copy-start | bytes 172036
  203.8 185.3 %copy-start.2 = (f32[16,896]{1,0:T(8,128)S(1)}, f32[16,896]{1,0:T(8,128)}, u32[]{:S(2)}) copy-start(f32[16,896]{1,0:T(8,128)} %param.10) | copy-start | bytes 172036
Sparse Core Ops, SparseCore 0:
  11.4 136.6 all-gather.2
  150.2 162.9 all-gather.4
  316.0 72.9 reduce-scatter.1
where the time goes:
time: 465 us; the launch traced here: 464 us
  blocking collectives  254 us (55%)
  waiting for transfers between devices  179 us (38%)
  matrix products  15.7 us (3%)
  between operations  13.8 us (3%)
    psum x1, blocking collectives, body(): projected = lax.psum(partial_proj, 'dp').astype(jnp.bfloat16)  188 us
    all_gather x1, waiting for transfers between devices, body(): weight_full = lax.all_gather(weight, 'fsdp', axis=1, tiled=True)  109 us
    reduce_scatter x1, waiting for transfers between devices, body(): lax.psum_scatter(grad_part, 'fsdp', scatter_dimension=1, tiled=True)  67.9 us
    all_gather x1, blocking collectives, body(): lax.all_gather(direction, 'dp', axis=0, tiled=True)  66.4 us
  transfers between devices with their start and end apart: 3, of which 2 were waited for; matrix products, arithmetic and copies ran while one was open for 3% of the time, Pallas kernels for 0%

commit v1 on v0

v1 whole, which is shorter than its diff:
```python
import jax
import jax.numpy as jnp
from jax import lax
from jax.experimental import pallas as pl
from jax.experimental.pallas import tpu as pltpu
from jax.sharding import PartitionSpec as P

decay_first = 0.9
decay_second = 0.999
bias_first = 0.9999734386
bias_second = 0.0952078528
epsilon_value = 1e-08

MESH = pl.DeviceIdType.MESH
BF16 = jnp.bfloat16
F32 = jnp.float32

ORDER = (
    (0, 0), (0, 1), (0, 2), (0, 3), (1, 0), (0, 4), (1, 1), (0, 5),
    (1, 2), (0, 6), (1, 3), (0, 7), (1, 4), (1, 5), (1, 6), (1, 7),
)
LAG = 5
HALF = 448
PART = 224


def remote(src, dst, send, recv, device):
    return pltpu.make_async_remote_copy(
        src_ref=src,
        dst_ref=dst,
        send_sem=send,
        recv_sem=recv,
        device_id=device,
        device_id_type=MESH,
    )


def landed(ref, sem):
    pltpu.make_async_copy(ref, ref, sem).wait()


def kernel(
    inputs, cotangent, weight, projector, first, second, grad_out, update_out,
    ring, blocks, weights, total, grads, part, part_in, pair, half_out, half_in, shares, shares_in, projected,
    grads_out, grads_in, sums_out, sums_in, direction,
    h_send, ring_recv, ring_send, x_send, x_recv, sib_send, sib_recv, w_send, w_recv,
    p_send, p_recv, ph_send, ph_recv, pz_send, pz_recv, px_send, px_recv,
    g_send, g_recv, c_send, c_recv, dh_send, d_recv, d_send, ds_send, ds_recv,
):
    j = lax.axis_index("dp")
    i = lax.axis_index("fsdp")
    x, l = i // 4, i % 4
    h, z, c = j // 16, (j // 2) % 8, j % 2

    def at(x=x, l=l, h=h, z=z, c=c):
        return {"dp": h * 16 + z * 2 + c, "fsdp": x * 4 + l}

    sibling = at(c=1 - c)
    partner = at(h=1 - h)
    right, left = at(z=(z + 1) % 8), at(z=(z + 7) % 8)

    barrier = pltpu.get_barrier_semaphore()
    peers = [sibling, partner]
    peers += [at(z=(z + k) % 8) for k in range(1, 8)]
    peers += [at(x=(x + k) % 4) for k in range(1, 4)]
    peers += [at(l=(l + k) % 4) for k in range(1, 4)]
    for peer in peers:
        pl.semaphore_signal(barrier, inc=1, device_id=peer, device_id_type=MESH)
    ring[0, z] = cotangent[...]
    weights[l] = weight[...]
    total[...] = jnp.zeros_like(total)
    grads[...] = jnp.zeros_like(grads)
    pl.semaphore_wait(barrier, len(peers))

    for s in range(2):
        rows = pl.ds(s * PART, PART)
        remote(ring.at[0, z, rows], ring.at[1, z, rows], h_send.at[s], ring_recv.at[1, z, s], partner).start()

    def place(q, o):
        dist = (o + 1) // 2
        zf = (z + 8 - dist) % 8 if o % 2 else (z + dist) % 8
        hf = h if q == 0 else 1 - h
        return dist, zf, 2 * hf + zf // 4, zf % 4

    def relay(q, o):
        dist, zf, xf, lf = place(q, o)
        for s in range(2):
            rows = pl.ds(s * PART, PART)
            piece = ring.at[q, zf, rows]
            if (q, o) != (0, 0):
                landed(piece, ring_recv.at[q, zf, s])
            if o == 0 or (o % 2 == 1 and dist + 1 <= 4 - s):
                remote(piece, piece, ring_send.at[q, 0, dist, s], ring_recv.at[q, zf, s], right).start()
            if o == 0 or (o % 2 == 0 and dist + 1 <= 3 + s):
                remote(piece, piece, ring_send.at[q, 1, dist, s], ring_recv.at[q, zf, s], left).start()

            @pl.when(xf != x)
            def _():
                there = blocks.at[lf, x, pl.ds(c * HALF + s * PART, PART)]
                remote(piece, there, x_send.at[q, o, s], x_recv.at[lf, x, s], at(x=xf)).start()

        @pl.when(xf == x)
        def _():
            there = blocks.at[lf, x, pl.ds(c * HALF, HALF)]
            remote(ring.at[q, zf], there, sib_send.at[lf, x], sib_recv.at[lf, x], sibling).start()
            blocks[lf, x, pl.ds(c * HALF, HALF)] = ring[q, zf]

    def share(q, o):
        _, _, xf, lf = place(q, o)

        @pl.when(xf == x)
        def _():
            for k in range(1, 4):
                xt = (x + k) % 4
                for s in range(2):
                    landed(blocks.at[lf, xt, pl.ds(c * HALF + s * PART, PART)], x_recv.at[lf, xt, s])
                mine = blocks.at[lf, xt, pl.ds(c * HALF, HALF)]
                remote(mine, mine, sib_send.at[lf, xt], sib_recv.at[lf, xt], sibling).start()

    def send_weight(origin, way):
        block = weights.at[origin]
        target = at(l=l + 1) if way == 0 else at(l=l - 1)
        return remote(block, block, w_send.at[way, origin], w_recv.at[origin], target)

    def pass_weight(step):
        @pl.when(l >= step)
        def _():
            if step:
                landed(weights.at[l - step], w_recv.at[l - step])

            @pl.when(l < 3)
            def _():
                send_weight(l - step, 0).start()

        @pl.when(l + step <= 3)
        def _():
            if step:
                landed(weights.at[l + step], w_recv.at[l + step])

            @pl.when(l > 0)
            def _():
                send_weight(l + step, 1).start()

    def project_pair():
        product = jnp.dot(inputs[...], projector[...], preferred_element_type=F32)
        part[...] = product.T.reshape(part.shape)
        remote(part.at[:, :, 1 - c], part_in, p_send, p_recv, sibling).start()

    def project_half():
        landed(part_in, p_recv)
        pair[...] = part[:, :, c] + part_in[...]
        half_out[...] = pair[1 - h].astype(BF16)
        remote(half_out, half_in, ph_send, ph_recv, partner).start()

    def project_share():
        landed(half_in, ph_recv)
        pair[h] = pair[h] + half_in[...].astype(F32)
        shares[...] = pair[h].astype(BF16)
        for k in range(1, 8):
            zp = (z + k) % 8
            remote(shares.at[zp], shares_in.at[z], pz_send.at[zp], pz_recv.at[z], at(z=zp)).start()

    def project_own():
        own = pair[h, z]
        for k in range(1, 8):
            zp = (z + k) % 8
            landed(shares_in.at[zp], pz_recv.at[zp])
            own = own + shares_in[zp].astype(F32)
        projected[x] = own.astype(BF16)
        for k in range(1, 4):
            xp = (x + k) % 4
            remote(projected.at[x], projected.at[x], px_send.at[xp], px_recv.at[x], at(x=xp)).start()

    for n, (q, o) in enumerate(ORDER):
        relay(q, o)
        if n >= LAG:
            share(*ORDER[n - LAG])
        if n == 0:
            project_pair()
        if n == 1:
            pass_weight(0)
            project_half()
        if n == 4:
            project_share()
        if n == 6:
            project_own()
            pass_weight(1)
        if n == 11:
            pass_weight(2)
    for n in range(16 - LAG, 16):
        share(*ORDER[n])

    @pl.when(l == 3)
    def _():
        landed(weights.at[0], w_recv.at[0])

    @pl.when(l == 0)
    def _():
        landed(weights.at[3], w_recv.at[3])

    for k in range(1, 4):
        xp = (x + k) % 4
        landed(projected.at[xp], px_recv.at[xp])

    def multiply(n, carry):
        lf, xt = n // 4, n % 4
        landed(blocks.at[lf, xt, pl.ds((1 - c) * HALF, HALF)], sib_recv.at[lf, xt])
        block = blocks[lf, xt]
        total[xt] += jnp.dot(weights[lf], block, preferred_element_type=F32)
        grads[lf] += lax.dot_general(
            projected[xt], block, (((1,), (1,)), ((), ())), preferred_element_type=F32
        )
        return carry

    lax.fori_loop(0, 16, multiply, 0)

    for k in range(1, 4):
        lp = (l + k) % 4
        grads_out[lp] = grads[lp].astype(BF16)
        remote(grads_out.at[lp], grads_in.at[l], g_send.at[lp], g_recv.at[l], at(l=lp)).start()
    for k in range(1, 4):
        xp = (x + k) % 4
        sums_out[xp] = total[xp].astype(BF16)
        remote(sums_out.at[xp], sums_in.at[x], c_send.at[xp], c_recv.at[x], at(x=xp)).start()

    gradient = grads[l]
    for k in range(1, 4):
        lp = (l + k) % 4
        landed(grads_in.at[lp], g_recv.at[lp])
        gradient = gradient + grads_in[lp].astype(F32)
    moment_one = decay_first * first[...] + (1.0 - decay_first) * gradient
    moment_two = decay_second * second[...] + (1.0 - decay_second) * gradient * gradient
    direction[h, z, c] = (
        moment_one / bias_first / (jnp.sqrt(moment_two / bias_second) + epsilon_value)
    ).astype(BF16)

    mine = direction.at[h, z, c]
    remote(mine, mine, dh_send, d_recv.at[1, z], partner).start()
    for q, o in ORDER:
        dist, zf, _, _ = place(q, o)
        hf = h if q == 0 else 1 - h
        piece = direction.at[hf, zf, c]
        if (q, o) != (0, 0):
            landed(piece, d_recv.at[q, zf])
        if o == 0 or (o % 2 == 1 and dist + 1 <= 4 - q):
            remote(piece, piece, d_send.at[q, 0, dist], d_recv.at[q, zf], right).start()
        if o == 0 or (o % 2 == 0 and dist + 1 <= 3 + q):
            remote(piece, piece, d_send.at[q, 1, dist], d_recv.at[q, zf], left).start()
    both = direction.at[:, :, c]
    remote(both, both, ds_send, ds_recv, sibling).start()

    result = total[x]
    for k in range(1, 4):
        xp = (x + k) % 4
        landed(sums_in.at[xp], c_recv.at[xp])
        result = result + sums_in[xp].astype(F32)
    grad_out[...] = result.T.astype(BF16)

    landed(direction.at[:, :, 1 - c], ds_recv)
    update_out[...] = jnp.dot(
        projector[...], direction[...].reshape(512, 896), preferred_element_type=F32
    ).astype(BF16)

    for s in range(2):
        landed(ring.at[0, z, pl.ds(s * PART, PART)], h_send.at[s])
    for q, o in ORDER:
        dist, zf, xf, lf = place(q, o)
        for s in range(2):
            piece = ring.at[q, zf, pl.ds(s * PART, PART)]
            if o == 0 or (o % 2 == 1 and dist + 1 <= 4 - s):
                landed(piece, ring_send.at[q, 0, dist, s])
            if o == 0 or (o % 2 == 0 and dist + 1 <= 3 + s):
                landed(piece, ring_send.at[q, 1, dist, s])

            @pl.when(xf != x)
            def _():
                landed(piece, x_send.at[q, o, s])

        if o == 0 or (o % 2 == 1 and dist + 1 <= 4 - q):
            landed(direction.at[h, zf, c], d_send.at[q, 0, dist])
        if o == 0 or (o % 2 == 0 and dist + 1 <= 3 + q):
            landed(direction.at[h, zf, c], d_send.at[q, 1, dist])
    for lf in range(4):
        for xt in range(4):
            landed(blocks.at[lf, xt, pl.ds(c * HALF, HALF)], sib_send.at[lf, xt])
    for step in range(3):

        @pl.when((l >= step) & (l < 3))
        def _():
            send_weight(l - step, 0).wait_send()

        @pl.when((l + step <= 3) & (l > 0))
        def _():
            send_weight(l + step, 1).wait_send()

    landed(part_in, p_send)
    landed(half_out, ph_send)
    for k in range(1, 8):
        zp = (z + k) % 8
        landed(shares.at[zp], pz_send.at[zp])
    for k in range(1, 4):
        xp, lp = (x + k) % 4, (l + k) % 4
        landed(projected.at[x], px_send.at[xp])
        landed(grads_out.at[lp], g_send.at[lp])
        landed(sums_out.at[xp], c_send.at[xp])
    landed(mine, dh_send)
    landed(both, ds_send)


def body(inputs, cotangent, weight, projector, first_moment, second_moment):
    dma = pltpu.SemaphoreType.DMA
    vmem = pl.BlockSpec(memory_space=pltpu.VMEM)
    return pl.pallas_call(
        kernel,
        out_shape=(
            jax.ShapeDtypeStruct((256, 256), BF16),
            jax.ShapeDtypeStruct((256, 896), BF16),
        ),
        in_specs=[vmem] * 6,
        out_specs=(vmem, vmem),
        scratch_shapes=[
            pltpu.VMEM((2, 8, 448, 256), BF16),
            pltpu.VMEM((4, 4, 896, 256), BF16),
            pltpu.VMEM((4, 256, 896), BF16),
            pltpu.VMEM((4, 256, 256), F32),
            pltpu.VMEM((4, 16, 896), F32),
            pltpu.VMEM((2, 8, 2, 16, 256), F32),
            pltpu.VMEM((2, 8, 16, 256), F32),
            pltpu.VMEM((2, 8, 16, 256), F32),
            pltpu.VMEM((8, 16, 256), BF16),
            pltpu.VMEM((8, 16, 256), BF16),
            pltpu.VMEM((8, 16, 256), BF16),
            pltpu.VMEM((8, 16, 256), BF16),
            pltpu.VMEM((4, 16, 256), BF16),
            pltpu.VMEM((4, 16, 896), BF16),
            pltpu.VMEM((4, 16, 896), BF16),
            pltpu.VMEM((4, 256, 256), BF16),
            pltpu.VMEM((4, 256, 256), BF16),
            pltpu.VMEM((2, 8, 2, 16, 896), BF16),
            dma((2,)), dma((2, 8, 2)), dma((2, 2, 4, 2)), dma((2, 8, 2)), dma((4, 4, 2)),
            dma((4, 4)), dma((4, 4)), dma((2, 4)), dma((4,)),
            dma(()), dma(()), dma(()), dma(()), dma((8,)), dma((8,)), dma((4,)), dma((4,)),
            dma((4,)), dma((4,)), dma((4,)), dma((4,)), dma(()), dma((2, 8)), dma((2, 2, 4)), dma(()), dma(()),
        ],
        compiler_params=pltpu.CompilerParams(
            collective_id=0, has_side_effects=True, vmem_limit_bytes=48 * 2**20
        ),
        cost_estimate=pl.CostEstimate(
            flops=2_300_000_000, bytes_accessed=2_000_000, transcendentals=28_672
        ),
        name="step",
    )(inputs, cotangent.T, weight, projector, first_moment, second_moment)


def solution(mesh):
    return jax.shard_map(
        body,
        mesh=mesh,
        in_specs=(
            P("fsdp", "dp"),
            P("fsdp", "dp"),
            P("dp", "fsdp"),
            P("dp", None),
            P("dp", "fsdp"),
            P("dp", "fsdp"),
        ),
        out_specs=(P("fsdp", "dp"), P("dp", "fsdp")),
        check_vma=False,
    )
```

time: 465 us -> 140 us (0.30)
  blocking collectives: 254 us -> 0 us
  waiting for transfers between devices: 179 us -> 0 us
  Pallas kernels: 0 us -> 131 us
  matrix products: 15.7 us -> 0 us
  between operations: 13.8 us -> 0.65 us
  local copies, waits for them, and re-layouts: 1 us -> 6.86 us
    psum x1 -> x0, blocking collectives: 188 us -> none  [body(): projected = lax.psum(partial_proj, 'dp').astype(jnp.bfloat16)]
    pallas_call x0 -> x1, Pallas kernels: none -> 131 us  [body(): pl.pallas_call(kernel, out_shape=(jax.ShapeDtypeStruct((256, 256), BF16),...]
    all_gather x2 -> x0, waiting for transfers between devices: 109 us -> none  [the longest x1 109 us: body(): weight_full = lax.all_gather(weight, 'fsdp', axis=1, tiled=True)]
    reduce_scatter x1 -> x0, waiting for transfers between devices: 67.9 us -> none  [body(): lax.psum_scatter(grad_part, 'fsdp', scatter_dimension=1, tiled=True)]
    all_gather x1 -> x0, blocking collectives: 66.4 us -> none  [body(): lax.all_gather(direction, 'dp', axis=0, tiled=True)]
    dot_general x4 -> x0, matrix products: 15.7 us -> none  [the longest x1 7.94 us: contract_cols(): lax.dot_general(left, right, (((1,), (1,)), ((), ())), preferred_element_...]
    unnamed x7 -> x14, local copies, waits for them, and re-layouts: 1 us -> 6.86 us
  transfers between devices with their start and end apart: 3 -> 0, of which waited for: 2 -> 0; matrix products, arithmetic and copies ran while one was open for 3% -> 0% of each run, Pallas kernels for 0% -> 0%
where the time goes in v1:
time: 140 us; the launch traced here: 139 us
  Pallas kernels  131 us (94%)
  local copies, waits for them, and re-layouts  6.86 us (5%)
    pallas_call x1, Pallas kernels, body(): pl.pallas_call(kernel, out_shape=(jax.ShapeDtypeStruct((256, 256), BF16),...  131 us
    unnamed x14, local copies, waits for them, and re-layouts  6.86 us

profile of v1, /device:TPU:1, one launch (start us, length us, event | category | flops | bytes accessed | tf_op | source)
XLA Modules:
  0.0 138.6 jit_solution(17497991619074551713)
XLA Ops:
  0.6 0.0 copy-start
  0.6 1.0 copy-done
  1.7 0.0 copy-start.1
  1.7 0.9 copy-done.1
  2.6 0.0 copy-start.2
  2.6 0.9 copy-done.2
  3.5 0.0 copy-start.3
  3.5 0.9 copy-done.3
  4.4 0.0 copy-start.4
  4.4 0.8 copy-done.4
  5.3 0.0 copy-start.5
  5.3 0.8 copy-done.5
  6.1 131.1 %step.1 = (bf16[256,256]{1,0:T(8,128)(2,1)S(1)}, bf16[256,896]{1,0:T(8,128)(2,1)S(1)}) custom-call(bf16[256,256]{1,0:T(8,128)(2,1)S(1)} %copy-done.3, bf16[448,256]{1,0:T(8,128)(2,1)S(1)} %bitcast.1, bf16[256,896]{1,0:T(8,128)(2,1)S(1)} %copy-done, bf16[256,512]{1,0:T(8,128)(2,1)S(1)} %copy-done.1, f32[16,896]{1,0:T(8,128)S(1)} %copy-done.4, ...), custom_call_target="tpu_custom_call" | custom-call | flops 2300000000 | bytes 2000000 | tf_op jit(solution)/shard_map/step/pallas_call | solution.py:313
  137.1 0.7 copy.10
  137.8 0.8 copy.11
Async XLA Ops:
  0.6 1.0 copy-start
  1.7 0.9 copy-start.1
  2.6 0.9 copy-start.2
  3.5 0.9 copy-start.3
  4.4 0.8 copy-start.4
  5.3 0.8 copy-start.5

commit v2 on v1

--- a/solution.py
+++ b/solution.py
@@ -16,10 +16,9 @@
 F32 = jnp.float32
 
 ORDER = (
-    (0, 0), (0, 1), (0, 2), (0, 3), (1, 0), (0, 4), (1, 1), (0, 5),
-    (1, 2), (0, 6), (1, 3), (0, 7), (1, 4), (1, 5), (1, 6), (1, 7),
+    (0, 0), (0, 1), (0, 2), (1, 0), (0, 3), (1, 1), (0, 4), (1, 2),
+    (0, 5), (1, 3), (0, 6), (1, 4), (0, 7), (1, 5), (1, 6), (1, 7),
 )
-LAG = 5
 HALF = 448
 PART = 224
 
@@ -40,10 +39,10 @@
 
 
 def kernel(
-    inputs, cotangent, weight, projector, first, second, grad_out, update_out,
-    ring, blocks, weights, total, grads, part, part_in, pair, half_out, half_in, shares, shares_in, projected,
+    inputs_hbm, cotangent_hbm, weight_hbm, projector_hbm, first_hbm, second_hbm, grad_out, update_out,
+    inputs, projector, first, second, ring, blocks, weights, total, grads, part, part_in, pair, half_out, half_in, shares, shares_in, projected,
     grads_out, grads_in, sums_out, sums_in, direction,
-    h_send, ring_recv, ring_send, x_send, x_recv, sib_send, sib_recv, w_send, w_recv,
+    load, h_send, ring_recv, ring_send, x_send, x_recv, sib_send, sib_recv, w_send, w_recv,
     p_send, p_recv, ph_send, ph_recv, pz_send, pz_recv, px_send, px_recv,
     g_send, g_recv, c_send, c_recv, dh_send, d_recv, d_send, ds_send, ds_recv,
 ):
@@ -59,6 +58,13 @@
     partner = at(h=1 - h)
     right, left = at(z=(z + 1) % 8), at(z=(z + 7) % 8)
 
+    def fetch(n):
+        src, dst = (
+            (cotangent_hbm, ring.at[0, z]), (inputs_hbm, inputs), (projector_hbm, projector),
+            (weight_hbm, weights.at[l]), (first_hbm, first), (second_hbm, second),
+        )[n]
+        return pltpu.make_async_copy(src, dst, load.at[n])
+
     barrier = pltpu.get_barrier_semaphore()
     peers = [sibling, partner]
     peers += [at(z=(z + k) % 8) for k in range(1, 8)]
@@ -66,10 +72,11 @@
     peers += [at(l=(l + k) % 4) for k in range(1, 4)]
     for peer in peers:
         pl.semaphore_signal(barrier, inc=1, device_id=peer, device_id_type=MESH)
-    ring[0, z] = cotangent[...]
-    weights[l] = weight[...]
+    for n in range(6):
+        fetch(n).start()
     total[...] = jnp.zeros_like(total)
     grads[...] = jnp.zeros_like(grads)
+    fetch(0).wait()
     pl.semaphore_wait(barrier, len(peers))
 
     for s in range(2):
@@ -105,17 +112,13 @@
             remote(ring.at[q, zf], there, sib_send.at[lf, x], sib_recv.at[lf, x], sibling).start()
             blocks[lf, x, pl.ds(c * HALF, HALF)] = ring[q, zf]
 
-    def share(q, o):
-        _, _, xf, lf = place(q, o)
-
-        @pl.when(xf == x)
-        def _():
-            for k in range(1, 4):
-                xt = (x + k) % 4
-                for s in range(2):
-                    landed(blocks.at[lf, xt, pl.ds(c * HALF + s * PART, PART)], x_recv.at[lf, xt, s])
-                mine = blocks.at[lf, xt, pl.ds(c * HALF, HALF)]
-                remote(mine, mine, sib_send.at[lf, xt], sib_recv.at[lf, xt], sibling).start()
+    def share(lf):
+        for k in range(1, 4):
+            xt = (x + k) % 4
+            for s in range(2):
+                landed(blocks.at[lf, xt, pl.ds(c * HALF + s * PART, PART)], x_recv.at[lf, xt, s])
+            mine = blocks.at[lf, xt, pl.ds(c * HALF, HALF)]
+            remote(mine, mine, sib_send.at[lf, xt], sib_recv.at[lf, xt], sibling).start()
 
     def send_weight(origin, way):
         block = weights.at[origin]
@@ -142,6 +145,8 @@
                 send_weight(l + step, 1).start()
 
     def project_pair():
+        fetch(1).wait()
+        fetch(2).wait()
         product = jnp.dot(inputs[...], projector[...], preferred_element_type=F32)
         part[...] = product.T.reshape(part.shape)
         remote(part.at[:, :, 1 - c], part_in, p_send, p_recv, sibling).start()
@@ -173,22 +178,25 @@
 
     for n, (q, o) in enumerate(ORDER):
         relay(q, o)
-        if n >= LAG:
-            share(*ORDER[n - LAG])
         if n == 0:
             project_pair()
         if n == 1:
+            project_half()
+        if n == 3:
+            project_share()
+        if n == 4:
+            fetch(3).wait()
             pass_weight(0)
-            project_half()
-        if n == 4:
-            project_share()
         if n == 6:
             project_own()
+        if n == 9:
             pass_weight(1)
-        if n == 11:
+        if n == 14:
             pass_weight(2)
-    for n in range(16 - LAG, 16):
-        share(*ORDER[n])
+
+    for k in range(1, 4):
+        xp = (x + k) % 4
+        landed(projected.at[xp], px_recv.at[xp])
 
     @pl.when(l == 3)
     def _():
@@ -198,31 +206,43 @@
     def _():
         landed(weights.at[3], w_recv.at[3])
 
-    for k in range(1, 4):
-        xp = (x + k) % 4
-        landed(projected.at[xp], px_recv.at[xp])
-
-    def multiply(n, carry):
-        lf, xt = n // 4, n % 4
-        landed(blocks.at[lf, xt, pl.ds((1 - c) * HALF, HALF)], sib_recv.at[lf, xt])
-        block = blocks[lf, xt]
-        total[xt] += jnp.dot(weights[lf], block, preferred_element_type=F32)
-        grads[lf] += lax.dot_general(
-            projected[xt], block, (((1,), (1,)), ((), ())), preferred_element_type=F32
-        )
+    def multiply(o, carry):
+        dist = (o + 1) // 2
+        zf = (z + jnp.where(o % 2 == 1, 8 - dist, dist)) % 8
+        lf = zf % 4
+
+        @pl.when(zf // 4 == x % 2)
+        def _():
+            share(lf)
+
+            def add(k, carry):
+                xt = (x + k) % 4
+                landed(blocks.at[lf, xt, pl.ds((1 - c) * HALF, HALF)], sib_recv.at[lf, xt])
+                block = blocks[lf, xt]
+                grads[lf] += lax.dot_general(
+                    projected[xt], block, (((1,), (1,)), ((), ())), preferred_element_type=F32
+                )
+                total[xt] += jnp.dot(weights[lf], block, preferred_element_type=F32)
+                return carry
+
+            lax.fori_loop(0, 4, add, 0)
+
+            @pl.when(lf != l)
+            def _():
+                grads_out[lf] = grads[lf].astype(BF16)
+                remote(grads_out.at[lf], grads_in.at[l], g_send.at[lf], g_recv.at[l], at(l=lf)).start()
+
         return carry
 
-    lax.fori_loop(0, 16, multiply, 0)
-
-    for k in range(1, 4):
-        lp = (l + k) % 4
-        grads_out[lp] = grads[lp].astype(BF16)
-        remote(grads_out.at[lp], grads_in.at[l], g_send.at[lp], g_recv.at[l], at(l=lp)).start()
+    lax.fori_loop(0, 8, multiply, 0)
+
     for k in range(1, 4):
         xp = (x + k) % 4
         sums_out[xp] = total[xp].astype(BF16)
         remote(sums_out.at[xp], sums_in.at[x], c_send.at[xp], c_recv.at[x], at(x=xp)).start()
 
+    fetch(4).wait()
+    fetch(5).wait()
     gradient = grads[l]
     for k in range(1, 4):
         lp = (l + k) % 4
@@ -316,9 +336,13 @@
             jax.ShapeDtypeStruct((256, 256), BF16),
             jax.ShapeDtypeStruct((256, 896), BF16),
         ),
-        in_specs=[vmem] * 6,
+        in_specs=[pl.BlockSpec(memory_space=pltpu.HBM)] * 6,
         out_specs=(vmem, vmem),
         scratch_shapes=[
+            pltpu.VMEM((256, 256), BF16),
+            pltpu.VMEM((256, 512), BF16),
+            pltpu.VMEM((16, 896), F32),
+            pltpu.VMEM((16, 896), F32),
             pltpu.VMEM((2, 8, 448, 256), BF16),
             pltpu.VMEM((4, 4, 896, 256), BF16),
             pltpu.VMEM((4, 256, 896), BF16),
@@ -337,13 +361,13 @@
             pltpu.VMEM((4, 256, 256), BF16),
             pltpu.VMEM((4, 256, 256), BF16),
             pltpu.VMEM((2, 8, 2, 16, 896), BF16),
-            dma((2,)), dma((2, 8, 2)), dma((2, 2, 4, 2)), dma((2, 8, 2)), dma((4, 4, 2)),
+            dma((6,)), dma((2,)), dma((2, 8, 2)), dma((2, 2, 4, 2)), dma((2, 8, 2)), dma((4, 4, 2)),
             dma((4, 4)), dma((4, 4)), dma((2, 4)), dma((4,)),
             dma(()), dma(()), dma(()), dma(()), dma((8,)), dma((8,)), dma((4,)), dma((4,)),
             dma((4,)), dma((4,)), dma((4,)), dma((4,)), dma(()), dma((2, 8)), dma((2, 2, 4)), dma(()), dma(()),
         ],
         compiler_params=pltpu.CompilerParams(
-            collective_id=0, has_side_effects=True, vmem_limit_bytes=48 * 2**20
+            collective_id=0, has_side_effects=True, vmem_limit_bytes=56000 * 1024
         ),
         cost_estimate=pl.CostEstimate(
             flops=2_300_000_000, bytes_accessed=2_000_000, transcendentals=28_672

time: 140 us -> 119 us (0.85)
  Pallas kernels: 131 us -> 114 us
  local copies, waits for them, and re-layouts: 6.86 us -> 3.39 us
    pallas_call x1, Pallas kernels: 131 us -> 114 us  [body(): pl.pallas_call(kernel, out_shape=(jax.ShapeDtypeStruct((256, 256), BF16),...]
    unnamed x14 -> x2, local copies, waits for them, and re-layouts: 6.86 us -> 3.39 us
where the time goes in v2:
time: 119 us; the launch traced here: 118 us
  Pallas kernels  114 us (96%)
  local copies, waits for them, and re-layouts  3.39 us (3%)
    pallas_call x1, Pallas kernels, body(): pl.pallas_call(kernel, out_shape=(jax.ShapeDtypeStruct((256, 256), BF16),...  114 us
    unnamed x2, local copies, waits for them, and re-layouts  3.39 us

profile of v2, /device:TPU:1, one launch (start us, length us, event | category | flops | bytes accessed | tf_op | source)
XLA Modules:
  0.0 118.2 jit_solution(7118870747739488731)
XLA Ops:
  0.6 114.2 %step.1 = (bf16[256,256]{1,0:T(8,128)(2,1)}, bf16[256,896]{1,0:T(8,128)(2,1)}) custom-call(bf16[256,256]{1,0:T(8,128)(2,1)} %inputs_hbm.1, bf16[448,256]{1,0:T(8,128)(2,1)} %bitcast.1, bf16[256,896]{1,0:T(8,128)(2,1)} %weight_hbm.1, bf16[256,512]{1,0:T(8,128)(2,1)} %projector_hbm.1, f32[16,896]{1,0:T(8,128)} %first_hbm.1, f32[16,896]{1,0:T(8,128)} %second_hbm.1), custom_call_target="tpu_custom_call" | custom-call | flops 2300000000 | bytes 2000000 | tf_op jit(solution)/shard_map/step/pallas_call | solution.py:333
  114.8 1.6 %copy.10 = bf16[256,256]{1,0:T(8,128)(2,1)} copy(bf16[256,256]{1,0:T(8,128)(2,1)} %get-tuple-element.4) | data formatting | bytes 262144
  116.4 1.8 %copy.11 = bf16[256,896]{1,0:T(8,128)(2,1)} copy(bf16[256,896]{1,0:T(8,128)(2,1)} %get-tuple-element.5) | data formatting | bytes 917504

commit v3 on v2

--- a/solution.py
+++ b/solution.py
@@ -16,8 +16,11 @@
 F32 = jnp.float32
 
 ORDER = (
-    (0, 0), (0, 1), (0, 2), (1, 0), (0, 3), (1, 1), (0, 4), (1, 2),
-    (0, 5), (1, 3), (0, 6), (1, 4), (0, 7), (1, 5), (1, 6), (1, 7),
+    (0, 0), (0, 1), (0, 2), (0, 3), (1, 0), (0, 4), (1, 1), (1, 2), (0, 5), (1, 3), (1, 4), (0, 6), (1, 5), (1, 6), (0, 7), (1, 7),
+)
+FIRST = ((0, 2), (0, -2), (1, 0), (1, 2), (1, -2), (0, 1), (0, -1))
+PASS = (
+    (0, -2, (1, 2)), (0, 2, (-1,)), (1, 0, (1, -1)), (1, -2, (1,)), (1, 2, (-1, -2)),
 )
 HALF = 448
 PART = 224
@@ -44,7 +47,7 @@
     grads_out, grads_in, sums_out, sums_in, direction,
     load, h_send, ring_recv, ring_send, x_send, x_recv, sib_send, sib_recv, w_send, w_recv,
     p_send, p_recv, ph_send, ph_recv, pz_send, pz_recv, px_send, px_recv,
-    g_send, g_recv, c_send, c_recv, dh_send, d_recv, d_send, ds_send, ds_recv,
+    g_send, g_recv, c_send, c_recv, d_recv, d_send, d_pass, ds_send, ds_recv,
 ):
     j = lax.axis_index("dp")
     i = lax.axis_index("fsdp")
@@ -68,6 +71,7 @@
     barrier = pltpu.get_barrier_semaphore()
     peers = [sibling, partner]
     peers += [at(z=(z + k) % 8) for k in range(1, 8)]
+    peers += [at(h=1 - h, z=(z + k) % 8) for k in (2, 6)]
     peers += [at(x=(x + k) % 4) for k in range(1, 4)]
     peers += [at(l=(l + k) % 4) for k in range(1, 4)]
     for peer in peers:
@@ -180,14 +184,14 @@
         relay(q, o)
         if n == 0:
             project_pair()
-        if n == 1:
+        if n == 2:
             project_half()
-        if n == 3:
+        if n == 7:
             project_share()
         if n == 4:
             fetch(3).wait()
             pass_weight(0)
-        if n == 6:
+        if n == 11:
             project_own()
         if n == 9:
             pass_weight(1)
@@ -254,18 +258,24 @@
         moment_one / bias_first / (jnp.sqrt(moment_two / bias_second) + epsilon_value)
     ).astype(BF16)
 
+    def hand_on(q, offset, steps):
+        hf = h if q == 0 else 1 - h
+        zf = (z + 8 + offset) % 8
+        piece = direction.at[hf, zf, c]
+        landed(piece, d_recv.at[q, zf])
+        for step in steps:
+            target = at(z=(z + 8 + step) % 8)
+            remote(piece, piece, d_pass.at[q, offset + 2, step + 2], d_recv.at[q, zf], target).start()
+
     mine = direction.at[h, z, c]
-    remote(mine, mine, dh_send, d_recv.at[1, z], partner).start()
-    for q, o in ORDER:
-        dist, zf, _, _ = place(q, o)
-        hf = h if q == 0 else 1 - h
-        piece = direction.at[hf, zf, c]
-        if (q, o) != (0, 0):
-            landed(piece, d_recv.at[q, zf])
-        if o == 0 or (o % 2 == 1 and dist + 1 <= 4 - q):
-            remote(piece, piece, d_send.at[q, 0, dist], d_recv.at[q, zf], right).start()
-        if o == 0 or (o % 2 == 0 and dist + 1 <= 3 + q):
-            remote(piece, piece, d_send.at[q, 1, dist], d_recv.at[q, zf], left).start()
+    for n, (q, step) in enumerate(FIRST):
+        target = at(h=h if q == 0 else 1 - h, z=(z + 8 + step) % 8)
+        remote(mine, mine, d_send.at[n], d_recv.at[q, z], target).start()
+    for q, offset, steps in PASS:
+        hand_on(q, offset, steps)
+    for q in range(2):
+        for offset in (-4, -3, -1, 1, 3):
+            hand_on(q, offset, ())
     both = direction.at[:, :, c]
     remote(both, both, ds_send, ds_recv, sibling).start()
 
@@ -295,11 +305,6 @@
             @pl.when(xf != x)
             def _():
                 landed(piece, x_send.at[q, o, s])
-
-        if o == 0 or (o % 2 == 1 and dist + 1 <= 4 - q):
-            landed(direction.at[h, zf, c], d_send.at[q, 0, dist])
-        if o == 0 or (o % 2 == 0 and dist + 1 <= 3 + q):
-            landed(direction.at[h, zf, c], d_send.at[q, 1, dist])
     for lf in range(4):
         for xt in range(4):
             landed(blocks.at[lf, xt, pl.ds(c * HALF, HALF)], sib_send.at[lf, xt])
@@ -323,7 +328,11 @@
         landed(projected.at[x], px_send.at[xp])
         landed(grads_out.at[lp], g_send.at[lp])
         landed(sums_out.at[xp], c_send.at[xp])
-    landed(mine, dh_send)
+    for n in range(len(FIRST)):
+        landed(mine, d_send.at[n])
+    for q, offset, steps in PASS:
+        for step in steps:
+            landed(mine, d_pass.at[q, offset + 2, step + 2])
     landed(both, ds_send)
 
 
@@ -364,7 +373,7 @@
             dma((6,)), dma((2,)), dma((2, 8, 2)), dma((2, 2, 4, 2)), dma((2, 8, 2)), dma((4, 4, 2)),
             dma((4, 4)), dma((4, 4)), dma((2, 4)), dma((4,)),
             dma(()), dma(()), dma(()), dma(()), dma((8,)), dma((8,)), dma((4,)), dma((4,)),
-            dma((4,)), dma((4,)), dma((4,)), dma((4,)), dma(()), dma((2, 8)), dma((2, 2, 4)), dma(()), dma(()),
+            dma((4,)), dma((4,)), dma((4,)), dma((4,)), dma((2, 8)), dma((7,)), dma((2, 5, 5)), dma(()), dma(()),
         ],
         compiler_params=pltpu.CompilerParams(
             collective_id=0, has_side_effects=True, vmem_limit_bytes=56000 * 1024

time: 119 us -> 110 us (0.924)
  the two profiles are of different devices: /device:TPU:1 before, /device:TPU:19 now
where the time goes in v3:
time: 110 us; the launch traced here: 109 us
  Pallas kernels  105 us (95%)
  local copies, waits for them, and re-layouts  3.39 us (3%)
    pallas_call x1, Pallas kernels, body(): pl.pallas_call(kernel, out_shape=(jax.ShapeDtypeStruct((256, 256), BF16),...  105 us
    unnamed x2, local copies, waits for them, and re-layouts  3.39 us

profile of v3, /device:TPU:19, one launch (start us, length us, event | category | flops | bytes accessed | tf_op | source)
XLA Modules:
  0.0 109.5 jit_solution(15010247398678944170)
XLA Ops:
  0.6 105.5 %step.1 = (bf16[256,256]{1,0:T(8,128)(2,1)}, bf16[256,896]{1,0:T(8,128)(2,1)}) custom-call(bf16[256,256]{1,0:T(8,128)(2,1)} %inputs_hbm.1, bf16[448,256]{1,0:T(8,128)(2,1)} %bitcast.1, bf16[256,896]{1,0:T(8,128)(2,1)} %weight_hbm.1, bf16[256,512]{1,0:T(8,128)(2,1)} %projector_hbm.1, f32[16,896]{1,0:T(8,128)} %first_hbm.1, f32[16,896]{1,0:T(8,128)} %second_hbm.1), custom_call_target="tpu_custom_call" | custom-call | flops 2300000000 | bytes 2000000 | tf_op jit(solution)/shard_map/step/pallas_call | solution.py:342
  106.1 1.6 %copy.10 = bf16[256,256]{1,0:T(8,128)(2,1)} copy(bf16[256,256]{1,0:T(8,128)(2,1)} %get-tuple-element.4) | data formatting | bytes 262144
  107.7 1.8 %copy.11 = bf16[256,896]{1,0:T(8,128)(2,1)} copy(bf16[256,896]{1,0:T(8,128)(2,1)} %get-tuple-element.5) | data formatting | bytes 917504

commit v4 on v3

--- a/solution.py
+++ b/solution.py
@@ -16,14 +16,15 @@
 F32 = jnp.float32
 
 ORDER = (
-    (0, 0), (0, 1), (0, 2), (0, 3), (1, 0), (0, 4), (1, 1), (1, 2), (0, 5), (1, 3), (1, 4), (0, 6), (1, 5), (1, 6), (0, 7), (1, 7),
+    (0, 0), (0, 1), (1, 0), (1, 1), (0, 2), (1, 2), (0, 3), (1, 3), (0, 4), (1, 4),
 )
 FIRST = ((0, 2), (0, -2), (1, 0), (1, 2), (1, -2), (0, 1), (0, -1))
 PASS = (
     (0, -2, (1, 2)), (0, 2, (-1,)), (1, 0, (1, -1)), (1, -2, (1,)), (1, 2, (-1, -2)),
 )
 HALF = 448
-PART = 224
+PARTS = 4
+PART = HALF // PARTS
 
 
 def remote(src, dst, send, recv, device):
@@ -83,43 +84,47 @@
     fetch(0).wait()
     pl.semaphore_wait(barrier, len(peers))
 
-    for s in range(2):
+    for s in range(PARTS):
         rows = pl.ds(s * PART, PART)
         remote(ring.at[0, z, rows], ring.at[1, z, rows], h_send.at[s], ring_recv.at[1, z, s], partner).start()
 
-    def place(q, o):
-        dist = (o + 1) // 2
-        zf = (z + 8 - dist) % 8 if o % 2 else (z + dist) % 8
+    def arrivals(q, dist):
         hf = h if q == 0 else 1 - h
-        return dist, zf, 2 * hf + zf // 4, zf % 4
-
-    def relay(q, o):
-        dist, zf, xf, lf = place(q, o)
-        for s in range(2):
-            rows = pl.ds(s * PART, PART)
-            piece = ring.at[q, zf, rows]
-            if (q, o) != (0, 0):
+        for s in range(PARTS):
+            limit = (4, 3) if s % 2 == 0 else (3, 4)
+            for way in range(2):
+                if dist > limit[way] or (dist == 0 and way == 1):
+                    continue
+                zf = (z + 8 - dist) % 8 if way == 0 else (z + dist) % 8
+                ways = (0, 1) if dist == 0 else (way,) if dist < limit[way] else ()
+                yield zf, 2 * hf + zf // 4, s, 2 * dist - way, ways
+
+    def relay(q, dist):
+        for zf, xf, s, o, ways in arrivals(q, dist):
+            piece = ring.at[q, zf, pl.ds(s * PART, PART)]
+            if (q, dist) != (0, 0):
                 landed(piece, ring_recv.at[q, zf, s])
-            if o == 0 or (o % 2 == 1 and dist + 1 <= 4 - s):
-                remote(piece, piece, ring_send.at[q, 0, dist, s], ring_recv.at[q, zf, s], right).start()
-            if o == 0 or (o % 2 == 0 and dist + 1 <= 3 + s):
-                remote(piece, piece, ring_send.at[q, 1, dist, s], ring_recv.at[q, zf, s], left).start()
+            for way in ways:
+                remote(piece, piece, ring_send.at[q, way, dist, s], ring_recv.at[q, zf, s], (right, left)[way]).start()
 
             @pl.when(xf != x)
             def _():
-                there = blocks.at[lf, x, pl.ds(c * HALF + s * PART, PART)]
-                remote(piece, there, x_send.at[q, o, s], x_recv.at[lf, x, s], at(x=xf)).start()
-
-        @pl.when(xf == x)
-        def _():
-            there = blocks.at[lf, x, pl.ds(c * HALF, HALF)]
-            remote(ring.at[q, zf], there, sib_send.at[lf, x], sib_recv.at[lf, x], sibling).start()
-            blocks[lf, x, pl.ds(c * HALF, HALF)] = ring[q, zf]
+                there = blocks.at[zf % 4, x, pl.ds(c * HALF + s * PART, PART)]
+                remote(piece, there, x_send.at[q, o, s], x_recv.at[zf % 4, x, s], at(x=xf)).start()
+
+        for zf in {0: [z], 4: [(z + 4) % 8]}.get(dist, [(z + 8 - dist) % 8, (z + dist) % 8]):
+            lf, xf = zf % 4, 2 * (h if q == 0 else 1 - h) + zf // 4
+
+            @pl.when(xf == x)
+            def _():
+                there = blocks.at[lf, x, pl.ds(c * HALF, HALF)]
+                remote(ring.at[q, zf], there, sib_send.at[lf, x], sib_recv.at[lf, x], sibling).start()
+                blocks[lf, x, pl.ds(c * HALF, HALF)] = ring[q, zf]
 
     def share(lf):
         for k in range(1, 4):
             xt = (x + k) % 4
-            for s in range(2):
+            for s in range(PARTS):
                 landed(blocks.at[lf, xt, pl.ds(c * HALF + s * PART, PART)], x_recv.at[lf, xt, s])
             mine = blocks.at[lf, xt, pl.ds(c * HALF, HALF)]
             remote(mine, mine, sib_send.at[lf, xt], sib_recv.at[lf, xt], sibling).start()
@@ -180,22 +185,22 @@
             xp = (x + k) % 4
             remote(projected.at[x], projected.at[x], px_send.at[xp], px_recv.at[x], at(x=xp)).start()
 
-    for n, (q, o) in enumerate(ORDER):
-        relay(q, o)
+    for n, (q, dist) in enumerate(ORDER):
+        relay(q, dist)
         if n == 0:
             project_pair()
+        if n == 1:
+            project_half()
+        if n == 4:
+            project_share()
         if n == 2:
-            project_half()
-        if n == 7:
-            project_share()
-        if n == 4:
             fetch(3).wait()
             pass_weight(0)
-        if n == 11:
+        if n == 7:
             project_own()
-        if n == 9:
+        if n == 5:
             pass_weight(1)
-        if n == 14:
+        if n == 8:
             pass_weight(2)
 
     for k in range(1, 4):
@@ -210,35 +215,40 @@
     def _():
         landed(weights.at[3], w_recv.at[3])
 
-    def multiply(o, carry):
+    def multiply(lf):
+        def add(k, carry):
+            xt = (x + k) % 4
+            landed(blocks.at[lf, xt, pl.ds((1 - c) * HALF, HALF)], sib_recv.at[lf, xt])
+            block = blocks[lf, xt]
+            grads[lf] += lax.dot_general(
+                projected[xt], block, (((1,), (1,)), ((), ())), preferred_element_type=F32
+            )
+            total[xt] += jnp.dot(weights[lf], block, preferred_element_type=F32)
+            return carry
+
+        lax.fori_loop(0, 4, add, 0)
+
+        @pl.when(lf != l)
+        def _():
+            grads_out[lf] = grads[lf].astype(BF16)
+            remote(grads_out.at[lf], grads_in.at[l], g_send.at[lf], g_recv.at[l], at(l=lf)).start()
+
+    def take(o, before):
         dist = (o + 1) // 2
         zf = (z + jnp.where(o % 2 == 1, 8 - dist, dist)) % 8
-        lf = zf % 4
-
-        @pl.when(zf // 4 == x % 2)
+        lf, mine = zf % 4, zf // 4 == x % 2
+
+        @pl.when(mine)
         def _():
             share(lf)
 
-            def add(k, carry):
-                xt = (x + k) % 4
-                landed(blocks.at[lf, xt, pl.ds((1 - c) * HALF, HALF)], sib_recv.at[lf, xt])
-                block = blocks[lf, xt]
-                grads[lf] += lax.dot_general(
-                    projected[xt], block, (((1,), (1,)), ((), ())), preferred_element_type=F32
-                )
-                total[xt] += jnp.dot(weights[lf], block, preferred_element_type=F32)
-                return carry
-
-            lax.fori_loop(0, 4, add, 0)
-
-            @pl.when(lf != l)
-            def _():
-                grads_out[lf] = grads[lf].astype(BF16)
-                remote(grads_out.at[lf], grads_in.at[l], g_send.at[lf], g_recv.at[l], at(l=lf)).start()
-
-        return carry
-
-    lax.fori_loop(0, 8, multiply, 0)
+        @pl.when(mine & (before >= 0))
+        def _():
+            multiply(before)
+
+        return jnp.where(mine, lf, before)
+
+    multiply(lax.fori_loop(0, 8, take, jnp.int32(-1)))
 
     for k in range(1, 4):
         xp = (x + k) % 4
@@ -291,20 +301,18 @@
         projector[...], direction[...].reshape(512, 896), preferred_element_type=F32
     ).astype(BF16)
 
-    for s in range(2):
+    for s in range(PARTS):
         landed(ring.at[0, z, pl.ds(s * PART, PART)], h_send.at[s])
-    for q, o in ORDER:
-        dist, zf, xf, lf = place(q, o)
-        for s in range(2):
+    for q, dist in ORDER:
+        for zf, xf, s, o, ways in arrivals(q, dist):
             piece = ring.at[q, zf, pl.ds(s * PART, PART)]
-            if o == 0 or (o % 2 == 1 and dist + 1 <= 4 - s):
-                landed(piece, ring_send.at[q, 0, dist, s])
-            if o == 0 or (o % 2 == 0 and dist + 1 <= 3 + s):
-                landed(piece, ring_send.at[q, 1, dist, s])
+            for way in ways:
+                landed(piece, ring_send.at[q, way, dist, s])
 
             @pl.when(xf != x)
             def _():
                 landed(piece, x_send.at[q, o, s])
+
     for lf in range(4):
         for xt in range(4):
             landed(blocks.at[lf, xt, pl.ds(c * HALF, HALF)], sib_send.at[lf, xt])
@@ -370,7 +378,7 @@
             pltpu.VMEM((4, 256, 256), BF16),
             pltpu.VMEM((4, 256, 256), BF16),
             pltpu.VMEM((2, 8, 2, 16, 896), BF16),
-            dma((6,)), dma((2,)), dma((2, 8, 2)), dma((2, 2, 4, 2)), dma((2, 8, 2)), dma((4, 4, 2)),
+            dma((6,)), dma((PARTS,)), dma((2, 8, PARTS)), dma((2, 2, 4, PARTS)), dma((2, 9, PARTS)), dma((4, 4, PARTS)),
             dma((4, 4)), dma((4, 4)), dma((2, 4)), dma((4,)),
             dma(()), dma(()), dma(()), dma(()), dma((8,)), dma((8,)), dma((4,)), dma((4,)),
             dma((4,)), dma((4,)), dma((4,)), dma((4,)), dma((2, 8)), dma((7,)), dma((2, 5, 5)), dma(()), dma(()),

time: 110 us -> 105 us (0.955)
  the two profiles are of different devices: /device:TPU:19 before, /device:TPU:1 now
where the time goes in v4:
time: 105 us
  Pallas kernels  101 us (96%)
  local copies, waits for them, and re-layouts  3.39 us (3%)
    pallas_call x1, Pallas kernels, body(): pl.pallas_call(kernel, out_shape=(jax.ShapeDtypeStruct((256, 256), BF16),...  101 us
    unnamed x2, local copies, waits for them, and re-layouts  3.39 us

profile of v4, /device:TPU:1, one launch (start us, length us, event | category | flops | bytes accessed | tf_op | source)
XLA Modules:
  0.0 104.8 jit_solution(9618331030642357080)
XLA Ops:
  0.6 100.8 %step.1 = (bf16[256,256]{1,0:T(8,128)(2,1)}, bf16[256,896]{1,0:T(8,128)(2,1)}) custom-call(bf16[256,256]{1,0:T(8,128)(2,1)} %inputs_hbm.1, bf16[448,256]{1,0:T(8,128)(2,1)} %bitcast.1, bf16[256,896]{1,0:T(8,128)(2,1)} %weight_hbm.1, bf16[256,512]{1,0:T(8,128)(2,1)} %projector_hbm.1, f32[16,896]{1,0:T(8,128)} %first_hbm.1, f32[16,896]{1,0:T(8,128)} %second_hbm.1), custom_call_target="tpu_custom_call" | custom-call | flops 2300000000 | bytes 2000000 | tf_op jit(solution)/shard_map/step/pallas_call | solution.py:350
  101.4 1.6 %copy.10 = bf16[256,256]{1,0:T(8,128)(2,1)} copy(bf16[256,256]{1,0:T(8,128)(2,1)} %get-tuple-element.4) | data formatting | bytes 262144
  103.0 1.8 %copy.11 = bf16[256,896]{1,0:T(8,128)(2,1)} copy(bf16[256,896]{1,0:T(8,128)(2,1)} %get-tuple-element.5) | data formatting | bytes 917504

commit v5 on v4

--- a/solution.py
+++ b/solution.py
@@ -43,12 +43,12 @@
 
 
 def kernel(
-    inputs_hbm, cotangent_hbm, weight_hbm, projector_hbm, first_hbm, second_hbm, grad_out, update_out,
+    inputs_hbm, cotangent_hbm, weight_hbm, projector_hbm, first_hbm, second_hbm, grad_out, direction_out,
     inputs, projector, first, second, ring, blocks, weights, total, grads, part, part_in, pair, half_out, half_in, shares, shares_in, projected,
     grads_out, grads_in, sums_out, sums_in, direction,
     load, h_send, ring_recv, ring_send, x_send, x_recv, sib_send, sib_recv, w_send, w_recv,
     p_send, p_recv, ph_send, ph_recv, pz_send, pz_recv, px_send, px_recv,
-    g_send, g_recv, c_send, c_recv, d_recv, d_send, d_pass, ds_send, ds_recv,
+    g_send, g_recv, c_send, c_recv, d_recv, d_send, d_pass, ds_send, ds_recv, store,
 ):
     j = lax.axis_index("dp")
     i = lax.axis_index("fsdp")
@@ -223,7 +223,6 @@
             grads[lf] += lax.dot_general(
                 projected[xt], block, (((1,), (1,)), ((), ())), preferred_element_type=F32
             )
-            total[xt] += jnp.dot(weights[lf], block, preferred_element_type=F32)
             return carry
 
         lax.fori_loop(0, 4, add, 0)
@@ -232,6 +231,12 @@
         def _():
             grads_out[lf] = grads[lf].astype(BF16)
             remote(grads_out.at[lf], grads_in.at[l], g_send.at[lf], g_recv.at[l], at(l=lf)).start()
+
+        def add_total(xt, carry):
+            total[xt] += jnp.dot(weights[lf], blocks[lf, xt], preferred_element_type=F32)
+            return carry
+
+        lax.fori_loop(0, 4, add_total, 0)
 
     def take(o, before):
         dist = (o + 1) // 2
@@ -283,24 +288,6 @@
         remote(mine, mine, d_send.at[n], d_recv.at[q, z], target).start()
     for q, offset, steps in PASS:
         hand_on(q, offset, steps)
-    for q in range(2):
-        for offset in (-4, -3, -1, 1, 3):
-            hand_on(q, offset, ())
-    both = direction.at[:, :, c]
-    remote(both, both, ds_send, ds_recv, sibling).start()
-
-    result = total[x]
-    for k in range(1, 4):
-        xp = (x + k) % 4
-        landed(sums_in.at[xp], c_recv.at[xp])
-        result = result + sums_in[xp].astype(F32)
-    grad_out[...] = result.T.astype(BF16)
-
-    landed(direction.at[:, :, 1 - c], ds_recv)
-    update_out[...] = jnp.dot(
-        projector[...], direction[...].reshape(512, 896), preferred_element_type=F32
-    ).astype(BF16)
-
     for s in range(PARTS):
         landed(ring.at[0, z, pl.ds(s * PART, PART)], h_send.at[s])
     for q, dist in ORDER:
@@ -309,10 +296,6 @@
             for way in ways:
                 landed(piece, ring_send.at[q, way, dist, s])
 
-            @pl.when(xf != x)
-            def _():
-                landed(piece, x_send.at[q, o, s])
-
     for lf in range(4):
         for xt in range(4):
             landed(blocks.at[lf, xt, pl.ds(c * HALF, HALF)], sib_send.at[lf, xt])
@@ -331,6 +314,33 @@
     for k in range(1, 8):
         zp = (z + k) % 8
         landed(shares.at[zp], pz_send.at[zp])
+    for q, dist in ORDER:
+        for zf, xf, s, o, _ in arrivals(q, dist):
+
+            @pl.when(xf != x)
+            def _():
+                landed(ring.at[q, zf, pl.ds(s * PART, PART)], x_send.at[q, o, s])
+
+    for q in range(2):
+        for offset in (-4, -3, -1, 1, 3):
+            hand_on(q, offset, ())
+    both = direction.at[:, :, c]
+    remote(both, both, ds_send, ds_recv, sibling).start()
+    pltpu.make_async_copy(both, direction_out.at[:, :, c], store.at[0]).start()
+
+    result = total[x]
+    for k in range(1, 4):
+        xp = (x + k) % 4
+        landed(sums_in.at[xp], c_recv.at[xp])
+        result = result + sums_in[xp].astype(F32)
+    grad_out[...] = result.T.astype(BF16)
+
+    other = direction.at[:, :, 1 - c]
+    landed(other, ds_recv)
+    pltpu.make_async_copy(other, direction_out.at[:, :, 1 - c], store.at[1]).start()
+    landed(other, store.at[1])
+    landed(both, store.at[0])
+
     for k in range(1, 4):
         xp, lp = (x + k) % 4, (l + k) % 4
         landed(projected.at[x], px_send.at[xp])
@@ -344,17 +354,24 @@
     landed(both, ds_send)
 
 
+def finish(grad, projector, direction, grad_out, update_out):
+    grad_out[...] = grad[...]
+    update_out[...] = jnp.dot(
+        projector[...], direction[...].reshape(512, 896), preferred_element_type=F32
+    ).astype(BF16)
+
+
 def body(inputs, cotangent, weight, projector, first_moment, second_moment):
     dma = pltpu.SemaphoreType.DMA
     vmem = pl.BlockSpec(memory_space=pltpu.VMEM)
-    return pl.pallas_call(
+    grad, direction = pl.pallas_call(
         kernel,
         out_shape=(
             jax.ShapeDtypeStruct((256, 256), BF16),
-            jax.ShapeDtypeStruct((256, 896), BF16),
+            jax.ShapeDtypeStruct((2, 8, 2, 16, 896), BF16),
         ),
         in_specs=[pl.BlockSpec(memory_space=pltpu.HBM)] * 6,
-        out_specs=(vmem, vmem),
+        out_specs=(vmem, pl.BlockSpec(memory_space=pltpu.HBM)),
         scratch_shapes=[
             pltpu.VMEM((256, 256), BF16),
             pltpu.VMEM((256, 512), BF16),
@@ -381,7 +398,7 @@
             dma((6,)), dma((PARTS,)), dma((2, 8, PARTS)), dma((2, 2, 4, PARTS)), dma((2, 9, PARTS)), dma((4, 4, PARTS)),
             dma((4, 4)), dma((4, 4)), dma((2, 4)), dma((4,)),
             dma(()), dma(()), dma(()), dma(()), dma((8,)), dma((8,)), dma((4,)), dma((4,)),
-            dma((4,)), dma((4,)), dma((4,)), dma((4,)), dma((2, 8)), dma((7,)), dma((2, 5, 5)), dma(()), dma(()),
+            dma((4,)), dma((4,)), dma((4,)), dma((4,)), dma((2, 8)), dma((7,)), dma((2, 5, 5)), dma(()), dma(()), dma((2,)),
         ],
         compiler_params=pltpu.CompilerParams(
             collective_id=0, has_side_effects=True, vmem_limit_bytes=56000 * 1024
@@ -391,6 +408,17 @@
         ),
         name="step",
     )(inputs, cotangent.T, weight, projector, first_moment, second_moment)
+    return pl.pallas_call(
+        finish,
+        out_shape=(
+            jax.ShapeDtypeStruct((256, 256), BF16),
+            jax.ShapeDtypeStruct((256, 896), BF16),
+        ),
+        in_specs=[vmem] * 3,
+        out_specs=(vmem, vmem),
+        compiler_params=pltpu.CompilerParams(vmem_limit_bytes=56000 * 1024),
+        name="finish",
+    )(grad, projector, direction)
 
 
 def solution(mesh):

time: 105 us -> 104 us (level); the launches traced: 105 us -> 102 us
  local copies, waits for them, and re-layouts: 3.39 us -> 0 us
    unnamed x2 -> x0, local copies, waits for them, and re-layouts: 3.39 us -> none
    pallas_call x0 -> x1, Pallas kernels: none -> 2.54 us  [body(): pl.pallas_call(finish, out_shape=(jax.ShapeDtypeStruct((256, 256), BF16),...]
    pallas_call x1, Pallas kernels: 101 us -> 98.9 us  [body(): pl.pallas_call(kernel, out_shape=(jax.ShapeDtypeStruct((256, 256), BF16),...]
where the time goes in v5:
time: 104 us; the launch traced here: 102 us
  Pallas kernels  101 us (97%)
    pallas_call x1, Pallas kernels, body(): pl.pallas_call(kernel, out_shape=(jax.ShapeDtypeStruct((256, 256), BF16),...  98.9 us
    pallas_call x1, Pallas kernels, body(): pl.pallas_call(finish, out_shape=(jax.ShapeDtypeStruct((256, 256), BF16),...  2.54 us

profile of v5, /device:TPU:1, one launch (start us, length us, event | category | flops | bytes accessed | tf_op | source)
XLA Modules:
  0.0 102.1 jit_solution(14805286679256424839)
XLA Ops:
  0.6 98.9 %step.1 = (bf16[256,256]{1,0:T(8,128)(2,1)}, bf16[2,8,2,16,896]{4,3,2,1,0:T(8,128)(2,1)}) custom-call(bf16[256,256]{1,0:T(8,128)(2,1)} %inputs_hbm.1, bf16[448,256]{1,0:T(8,128)(2,1)} %bitcast.1, bf16[256,896]{1,0:T(8,128)(2,1)} %weight_hbm.1, bf16[256,512]{1,0:T(8,128)(2,1)} %projector.1, f32[16,896]{1,0:T(8,128)} %first_hbm.1, f32[16,896]{1,0:T(8,128)} %second_hbm.1), custom_call_target="tpu_custom_call" | custom-call | flops 2300000000 | bytes 2000000 | tf_op jit(solution)/shard_map/step/pallas_call | solution.py:367
  99.6 2.5 %finish.1 = (bf16[256,256]{1,0:T(8,128)(2,1)}, bf16[256,896]{1,0:T(8,128)(2,1)}) custom-call(bf16[256,256]{1,0:T(8,128)(2,1)} %get-tuple-element.4.grad, bf16[256,512]{1,0:T(8,128)(2,1)} %projector.1, bf16[2,8,2,16,896]{4,3,2,1,0:T(8,128)(2,1)} %get-tuple-element.5.direction), custom_call_target="tpu_custom_call" | custom-call | tf_op jit(solution)/shard_map/finish/pallas_call | solution.py:411

commit v6 on v5

--- a/solution.py
+++ b/solution.py
@@ -324,10 +324,10 @@
     for q in range(2):
         for offset in (-4, -3, -1, 1, 3):
             hand_on(q, offset, ())
-    both = direction.at[:, :, c]
-    remote(both, both, ds_send, ds_recv, sibling).start()
-    pltpu.make_async_copy(both, direction_out.at[:, :, c], store.at[0]).start()
-
+        hf = h if q == 0 else 1 - h
+        half = direction.at[hf, :, c]
+        remote(half, half, ds_send.at[q], ds_recv.at[q], sibling).start()
+        pltpu.make_async_copy(half, direction_out.at[hf, :, c], store.at[0, q]).start()
     result = total[x]
     for k in range(1, 4):
         xp = (x + k) % 4
@@ -335,11 +335,14 @@
         result = result + sums_in[xp].astype(F32)
     grad_out[...] = result.T.astype(BF16)
 
-    other = direction.at[:, :, 1 - c]
-    landed(other, ds_recv)
-    pltpu.make_async_copy(other, direction_out.at[:, :, 1 - c], store.at[1]).start()
-    landed(other, store.at[1])
-    landed(both, store.at[0])
+    for q in range(2):
+        hf = h if q == 0 else 1 - h
+        other = direction.at[hf, :, 1 - c]
+        landed(other, ds_recv.at[q])
+        pltpu.make_async_copy(other, direction_out.at[hf, :, 1 - c], store.at[1, q]).start()
+    for q in range(2):
+        for n in range(2):
+            landed(direction.at[h, :, c], store.at[n, q])
 
     for k in range(1, 4):
         xp, lp = (x + k) % 4, (l + k) % 4
@@ -351,7 +354,8 @@
     for q, offset, steps in PASS:
         for step in steps:
             landed(mine, d_pass.at[q, offset + 2, step + 2])
-    landed(both, ds_send)
+    for q in range(2):
+        landed(direction.at[h, :, c], ds_send.at[q])
 
 
 def finish(grad, projector, direction, grad_out, update_out):
@@ -398,7 +402,7 @@
             dma((6,)), dma((PARTS,)), dma((2, 8, PARTS)), dma((2, 2, 4, PARTS)), dma((2, 9, PARTS)), dma((4, 4, PARTS)),
             dma((4, 4)), dma((4, 4)), dma((2, 4)), dma((4,)),
             dma(()), dma(()), dma(()), dma(()), dma((8,)), dma((8,)), dma((4,)), dma((4,)),
-            dma((4,)), dma((4,)), dma((4,)), dma((4,)), dma((2, 8)), dma((7,)), dma((2, 5, 5)), dma(()), dma(()), dma((2,)),
+            dma((4,)), dma((4,)), dma((4,)), dma((4,)), dma((2, 8)), dma((7,)), dma((2, 5, 5)), dma((2,)), dma((2,)), dma((2, 2)),
         ],
         compiler_params=pltpu.CompilerParams(
             collective_id=0, has_side_effects=True, vmem_limit_bytes=56000 * 1024

time: 104 us -> 103 us (level)
  no operation moved by 1% of the time
where the time goes in v6:
time: 103 us; the launch traced here: 102 us
  Pallas kernels  101 us (98%)
    pallas_call x1, Pallas kernels, body(): pl.pallas_call(kernel, out_shape=(jax.ShapeDtypeStruct((256, 256), BF16),...  98.5 us
    pallas_call x1, Pallas kernels, body(): pl.pallas_call(finish, out_shape=(jax.ShapeDtypeStruct((256, 256), BF16),...  2.54 us

profile of v6, /device:TPU:1, one launch (start us, length us, event | category | flops | bytes accessed | tf_op | source)
XLA Modules:
  0.0 101.7 jit_solution(5032581334449189617)
XLA Ops:
  0.6 98.5 %step.1 = (bf16[256,256]{1,0:T(8,128)(2,1)}, bf16[2,8,2,16,896]{4,3,2,1,0:T(8,128)(2,1)}) custom-call(bf16[256,256]{1,0:T(8,128)(2,1)} %inputs_hbm.1, bf16[448,256]{1,0:T(8,128)(2,1)} %bitcast.1, bf16[256,896]{1,0:T(8,128)(2,1)} %weight_hbm.1, bf16[256,512]{1,0:T(8,128)(2,1)} %projector.1, f32[16,896]{1,0:T(8,128)} %first_hbm.1, f32[16,896]{1,0:T(8,128)} %second_hbm.1), custom_call_target="tpu_custom_call" | custom-call | flops 2300000000 | bytes 2000000 | tf_op jit(solution)/shard_map/step/pallas_call | solution.py:371
  99.2 2.5 %finish.1 = (bf16[256,256]{1,0:T(8,128)(2,1)}, bf16[256,896]{1,0:T(8,128)(2,1)}) custom-call(bf16[256,256]{1,0:T(8,128)(2,1)} %get-tuple-element.4.grad, bf16[256,512]{1,0:T(8,128)(2,1)} %projector.1, bf16[2,8,2,16,896]{4,3,2,1,0:T(8,128)(2,1)} %get-tuple-element.5.direction), custom_call_target="tpu_custom_call" | custom-call | tf_op jit(solution)/shard_map/finish/pallas_call | solution.py:415
